TPU v7x, 32 devices: a whole 2x2x4 slice. The times are simulated.
32 devices in a mesh: orb: 8 (over y, x, core), probe: 4 (over z).
Axes of the slice: x: 2, y: 2, z: 4, core: 2. Of those that a mesh axis runs over, the one named last changes fastest.
Arguments:
- tiles: bfloat16 [32, 9, 256, 256], P('orb', None, 'probe'), may hold values from -0.0625 to 0.0625
- pattern: int32 [32, 9], P('orb'), may hold values from 0 to 1, as said below
- signs: int32 [8192, 512], P('orb', 'probe'), may hold values from 0 to 1
- previous: bfloat16 [8192, 512], P('orb', 'probe'), may hold values from -6 to 6
- current: bfloat16 [8192, 512], P('orb', 'probe'), may hold values from -6 to 6
Outputs:
- older: bfloat16 [8192, 512], P('orb', 'probe')
- newest: bfloat16 [8192, 512], P('orb', 'probe')
- moments: float32 [4, 512], P(None, 'probe')
Inputs may be any that keep to these rules, and one draw needn't show every extreme that they name: pattern[I, 4] is 1 for every row block; each row block has 4 to 9 ones; the 4 row blocks of one index of orb hold at most 28 ones together, and some index of orb holds exactly 28.
All inputs are finite; a program needn't handle non-finite values.
Results may differ from a plain program's by a relative error of at most 0.0053.
Values may be sent and summed in bfloat16 or wider, within the bound.
A program may use at most 64 MiB of HBM per device.

v0:
```python
import math
import jax
import jax.numpy as jnp
from jax import lax
from jax.sharding import PartitionSpec as P

REACH = 4
STEPS = 4


def extended(array, sides, width):
    for axis, dim in sides:
        peers, length = (lax.axis_size(axis), array.shape[dim])
        up = [(i, (i + 1) % peers) for i in range(peers)]
        down = [(j, i) for i, j in up]
        last = lax.slice_in_dim(array, length - width, length, axis=dim)
        initial = lax.slice_in_dim(array, 0, width, axis=dim)
        before = lax.ppermute(last, axis, up)
        after = lax.ppermute(initial, axis, down)
        array = jnp.concatenate([before, array, after], axis=dim)
    return array


def extend_panel(vec, block_rows):
    return extended(vec, (("orb", 0),), REACH * block_rows)


def body(tiles, pattern, signs, previous, current):
    row_blocks, offsets, shard_rows, block_rows = tiles.shape
    probe_count = previous.shape[1]
    sign_f = (2 * signs - 1).astype(jnp.float32)
    factor = 1.0 / math.sqrt(lax.axis_size("orb") * row_blocks * block_rows)
    full_tiles = lax.all_gather(tiles, "probe", axis=2, tiled=True)
    mask_b = pattern.astype(jnp.bfloat16)
    older, newest = (previous, current)
    collected = []
    for step in range(STEPS):
        blocks = extend_panel(newest, block_rows).reshape(
            row_blocks + 2 * REACH, block_rows, probe_count
        )
        windows = jnp.stack(
            [blocks[offset : offset + row_blocks] for offset in range(offsets)], axis=1
        )
        windows = windows * mask_b[:, :, None, None]
        total = jnp.einsum(
            "roij,rojp->rip", full_tiles, windows, preferred_element_type=jnp.float32
        )
        image = total.reshape(row_blocks * block_rows, probe_count)
        nxt = (2.0 * image - older.astype(jnp.float32)).astype(jnp.bfloat16)
        local_sum = jnp.sum(sign_f * nxt.astype(jnp.float32), axis=0)
        collected.append(lax.psum(local_sum, "orb") * factor)
        older, newest = (newest, nxt)
    stacked = jnp.stack(collected)
    return (older, newest, stacked)


def solution(mesh):
    placed = (
        P("orb", None, "probe", None),
        P("orb", None),
        P("orb", "probe"),
        P("orb", "probe"),
        P("orb", "probe"),
    )
    return jax.shard_map(
        body,
        mesh=mesh,
        in_specs=placed,
        out_specs=(P("orb", "probe"), P("orb", "probe"), P(None, "probe")),
        check_vma=False,
    )
```

profile of v0, /device:TPU:0, one launch (start us, length us, event | category | flops | bytes accessed | tf_op | source)
XLA Modules:
  0.0 224.4 jit_solution(14347151901448904519)
XLA Ops:
  8.4 2.9 %collective-permute-start.1 = (bf16[1024,128]{1,0:T(8,128)(2,1)}, bf16[1024,128]{1,0:T(8,128)(2,1)S(1)}, u32[]{:S(2)}, u32[]{:S(2)}) collective-permute-start(bf16[1024,128]{1,0:T(8,128)(2,1)} %param.9), channel_id=1, source_target_pairs={{4,0},{8,4},{12,8},{16,12},{20,16},{24,20},{28,24},{0,28},{5,1},{9... | collective-permute-start | bytes 786440 | tf_op jit(solution)/shard_map/ppermute | solution.py:19
  11.4 1.1 copy.48
  13.2 2.5 %collective-permute-done = bf16[1024,128]{1,0:T(8,128)(2,1)S(1)} collective-permute-done((bf16[1024,128]{1,0:T(8,128)(2,1)}, bf16[1024,128]{1,0:T(8,128)(2,1)S(1)}, u32[]{:S(2)}, u32[]{:S(2)}) %collective-permute-start) | collective-permute-done | bytes 262176 | tf_op jit(solution)/shard_map/ppermute | solution.py:18
  15.8 1.5 collective-permute-done.1
  23.0 1.1 constant_dynamic-update-slice_fusion.12
  24.1 1.0 constant_dynamic-update-slice_fusion.10
  25.3 76.4 %all-gather.2.cloned.1.call-done = bf16[4,9,256,256]{3,2,1,0:T(8,128)(2,1)} async-done(((bf16[4,9,64,256]{3,2,1,0:T(8,128)(2,1)}), bf16[4,9,256,256]{3,2,1,0:T(8,128)(2,1)}) %all-gather.2.cloned.1.call-update) | async-done | bytes 4718608 | tf_op jit(solution)/shard_map/all_gather | solution.py:33
  101.7 4.0 %fusion.41 = f32[4,256,128]{1,2,0:T(8,128)S(1)} fusion(bf16[4,9,256,256]{3,2,1,0:T(8,128)(2,1)} %all-gather.2.cloned.1.call-done, bf16[4,9,256,128]{2,3,1,0:T(8,128)(2,1)S(1)} %constant_dynamic-update-slice_fusion.4, bf16[4,9]{1,0:T(4,128)(2,1)S(1)} %convert_element_type.38), kind=kOutput, calls=%fused_computation.19 | convolution fusion | flops 605290496 | bytes 7602248 | tf_op jit(solution)/shard_map/roij,rojp->rip/dot_general | solution.py:45
  105.9 1.1 fusion.53
  107.0 2.6 %collective-permute-start.3 = (bf16[1024,128]{1,0:T(8,128)(2,1)S(1)}, bf16[1024,128]{1,0:T(8,128)(2,1)S(1)}, u32[]{:S(2)}, u32[]{:S(2)}) collective-permute-start(bf16[1024,128]{1,0:T(8,128)(2,1)S(1)} %fusion.53), channel_id=1, source_target_pairs={{4,0},{8,4},{12,8},{16,12},{20,16},{24,20},{28,24},{0,28},{5,1},{9... | collective-permute-start | bytes 786440 | tf_op jit(solution)/shard_map/ppermute | solution.py:19
  110.5 4.2 %collective-permute-done.2 = bf16[1024,128]{1,0:T(8,128)(2,1)S(1)} collective-permute-done((bf16[1024,128]{1,0:T(8,128)(2,1)S(1)}, bf16[1024,128]{1,0:T(8,128)(2,1)S(1)}, u32[]{:S(2)}, u32[]{:S(2)}) %collective-permute-start.2) | collective-permute-done | bytes 262176 | tf_op jit(solution)/shard_map/ppermute | solution.py:18
  114.7 1.0 pad_maximum_fusion.4
  118.4 1.8 copy.56
  120.2 1.8 copy.57
  122.0 1.8 copy.59
  123.8 1.8 copy.60
  126.6 1.0 constant_dynamic-update-slice_fusion.20
  127.7 1.0 constant_dynamic-update-slice_fusion.19
  129.6 1.0 constant_dynamic-update-slice_fusion.17
  130.6 1.0 constant_dynamic-update-slice_fusion.16
  131.7 4.0 %fusion.35 = f32[4,256,128]{1,2,0:T(8,128)S(1)} fusion(bf16[4,9,256,256]{3,2,1,0:T(8,128)(2,1)} %all-gather.2.cloned.1.call-done, bf16[4,9,256,128]{2,3,1,0:T(8,128)(2,1)S(1)} %constant_dynamic-update-slice_fusion.13, bf16[4,9]{1,0:T(4,128)(2,1)S(1)} %convert_element_type.38), kind=kOutput, calls=%fused_computation.17 | convolution fusion | flops 605290496 | bytes 7602248 | tf_op jit(solution)/shard_map/roij,rojp->rip/dot_general | solution.py:45
  135.9 1.7 collective-permute-start.4
  137.7 1.1 collective-permute-start.5
  139.6 4.7 %collective-permute-done.4 = bf16[1024,128]{1,0:T(8,128)(2,1)S(1)} collective-permute-done((bf16[1024,128]{1,0:T(8,128)(2,1)S(1)}, bf16[1024,128]{1,0:T(8,128)(2,1)S(1)}, u32[]{:S(2)}, u32[]{:S(2)}) %collective-permute-start.4) | collective-permute-done | bytes 262176 | tf_op jit(solution)/shard_map/ppermute | solution.py:18
  144.4 1.0 pad_maximum_fusion.2
  148.1 1.8 copy.66
  149.9 1.8 copy.67
  151.7 1.8 copy.69
  153.5 1.8 copy.70
  156.3 1.0 constant_dynamic-update-slice_fusion.29
  157.3 1.0 constant_dynamic-update-slice_fusion.28
  159.3 1.0 constant_dynamic-update-slice_fusion.26
  161.3 4.8 %fusion.29 = f32[4,256,128]{1,2,0:T(8,128)} fusion(bf16[4,9,256,256]{3,2,1,0:T(8,128)(2,1)} %all-gather.2.cloned.1.call-done, bf16[4,9,256,128]{2,3,1,0:T(8,128)(2,1)S(1)} %constant_dynamic-update-slice_fusion.22, bf16[4,9]{1,0:T(4,128)(2,1)S(1)} %convert_element_type.38), kind=kOutput, calls=%fused_computation.15 | convolution fusion | flops 605290496 | bytes 7602248 | tf_op jit(solution)/shard_map/roij,rojp->rip/dot_general | solution.py:45
  166.1 1.2 copy.73
  167.5 2.0 collective-permute-start.6
  171.0 5.2 %collective-permute-done.6 = bf16[1024,128]{1,0:T(8,128)(2,1)S(1)} collective-permute-done((bf16[1024,128]{1,0:T(8,128)(2,1)S(1)}, bf16[1024,128]{1,0:T(8,128)(2,1)S(1)}, u32[]{:S(2)}, u32[]{:S(2)}) %collective-permute-start.6) | collective-permute-done | bytes 262176 | tf_op jit(solution)/shard_map/ppermute | solution.py:18
  176.2 1.2 pad_maximum_fusion
  180.0 1.8 copy.76
  181.8 1.8 copy.77
  183.6 1.8 copy.79
  185.4 1.8 copy.80
  187.2 1.8 copy.81
  189.9 1.0 constant_dynamic-update-slice_fusion.38
  190.9 1.0 constant_dynamic-update-slice_fusion.37
  194.9 4.8 %fusion.23 = f32[4,256,128]{1,2,0:T(8,128)} fusion(bf16[4,9,256,256]{3,2,1,0:T(8,128)(2,1)} %all-gather.2.cloned.1.call-done, bf16[4,9,256,128]{2,3,1,0:T(8,128)(2,1)S(1)} %constant_dynamic-update-slice_fusion.31, bf16[4,9]{1,0:T(4,128)(2,1)S(1)} %convert_element_type.38), kind=kOutput, calls=%fused_computation.13 | convolution fusion | flops 605290496 | bytes 7602248 | tf_op jit(solution)/shard_map/roij,rojp->rip/dot_general | solution.py:45
  199.7 1.2 copy.83
  201.0 2.0 fusion.49
  203.0 13.9 %all-reduce = (f32[128]{0:T(128)S(1)}, f32[128]{0:T(128)S(1)}, f32[128]{0:T(128)S(1)}, f32[128]{0:T(128)S(1)}) all-reduce(f32[128]{0:T(128)S(1)} %get-tuple-element.4, f32[128]{0:T(128)S(1)} %get-tuple-element.5, f32[128]{0:T(128)S(1)} %get-tuple-element.6, f32[128]{0:T(128)S(1)} %get-tuple-element.3), channel_id=1, replica_groups=mesh['orb'=8,'probe'=4] {'orb'}, use_global_device_ids=true, to_apply=%region_7.0 | all-reduce | flops 512 | bytes 4096 | tf_op jit(solution)/shard_map/psum | solution.py:51
  (95 shorter events, 29.1 us)
Async XLA Ops:
  7.2 8.6 %copy-start.1 = (bf16[1024,128]{1,0:T(8,128)(2,1)S(1)}, bf16[1024,128]{1,0:T(8,128)(2,1)}, u32[]{:S(2)}) copy-start(bf16[1024,128]{1,0:T(8,128)(2,1)} %param.9) | copy-start | bytes 786436
  7.2 94.5 %all-gather.2.cloned.1.call-start = ((), (), s32[]{:S(2)}) async-start(), calls=%async_computation | async-start | bytes 5898240 | tf_op jit(solution)/shard_map/all_gather | solution.py:33
  7.9 7.8 %collective-permute-start = (bf16[1024,128]{1,0:T(8,128)(2,1)}, bf16[1024,128]{1,0:T(8,128)(2,1)S(1)}, u32[]{:S(2)}, u32[]{:S(2)}) collective-permute-start(bf16[1024,128]{1,0:T(8,128)(2,1)} %param.9), channel_id=1, source_target_pairs={{0,4},{4,8},{8,12},{12,16},{16,20},{20,24},{24,28},{28,0},{1,5},{5... | collective-permute-start | bytes 786440 | tf_op jit(solution)/shard_map/ppermute | solution.py:18
  8.4 8.9 %collective-permute-start.1 = (bf16[1024,128]{1,0:T(8,128)(2,1)}, bf16[1024,128]{1,0:T(8,128)(2,1)S(1)}, u32[]{:S(2)}, u32[]{:S(2)}) collective-permute-start(bf16[1024,128]{1,0:T(8,128)(2,1)} %param.9), channel_id=1, source_target_pairs={{4,0},{8,4},{12,8},{16,12},{20,16},{24,20},{28,24},{0,28},{5,1},{9... | collective-permute-start | bytes 786440 | tf_op jit(solution)/shard_map/ppermute | solution.py:19
  23.0 2.1 copy-start.5
  23.0 2.2 copy-start.3
  23.0 2.2 copy-start.4
  23.0 2.2 copy-start.2
  107.0 7.7 %collective-permute-start.2 = (bf16[1024,128]{1,0:T(8,128)(2,1)S(1)}, bf16[1024,128]{1,0:T(8,128)(2,1)S(1)}, u32[]{:S(2)}, u32[]{:S(2)}) collective-permute-start(bf16[1024,128]{1,0:T(8,128)(2,1)S(1)} %fusion.53), channel_id=1, source_target_pairs={{0,4},{4,8},{8,12},{12,16},{16,20},{20,24},{24,28},{28,0},{1,5},{5... | collective-permute-start | bytes 786440 | tf_op jit(solution)/shard_map/ppermute | solution.py:18
  107.0 7.7 %collective-permute-start.3 = (bf16[1024,128]{1,0:T(8,128)(2,1)S(1)}, bf16[1024,128]{1,0:T(8,128)(2,1)S(1)}, u32[]{:S(2)}, u32[]{:S(2)}) collective-permute-start(bf16[1024,128]{1,0:T(8,128)(2,1)S(1)} %fusion.53), channel_id=1, source_target_pairs={{4,0},{8,4},{12,8},{16,12},{20,16},{24,20},{28,24},{0,28},{5,1},{9... | collective-permute-start | bytes 786440 | tf_op jit(solution)/shard_map/ppermute | solution.py:19
  126.6 4.9 %copy-start.7 = (bf16[4,1,256,128]{2,3,1,0:T(8,128)(2,1)S(1)}, bf16[4,1,256,128]{2,3,1,0:T(8,128)(2,1)}, u32[]{:S(2)}) copy-start(bf16[4,1,256,128]{2,3,1,0:T(8,128)(2,1)} %copy.60) | copy-start | bytes 786436
  126.6 5.0 %copy-start.8 = (bf16[4,1,256,128]{2,3,1,0:T(8,128)(2,1)S(1)}, bf16[4,1,256,128]{2,3,1,0:T(8,128)(2,1)}, u32[]{:S(2)}) copy-start(bf16[4,1,256,128]{2,3,1,0:T(8,128)(2,1)} %copy.61) | copy-start | bytes 786436
  135.9 8.4 %collective-permute-start.4 = (bf16[1024,128]{1,0:T(8,128)(2,1)S(1)}, bf16[1024,128]{1,0:T(8,128)(2,1)S(1)}, u32[]{:S(2)}, u32[]{:S(2)}) collective-permute-start(bf16[1024,128]{1,0:T(8,128)(2,1)S(1)} %fusion.52), channel_id=1, source_target_pairs={{0,4},{4,8},{8,12},{12,16},{16,20},{20,24},{24,28},{28,0},{1,5},{5... | collective-permute-start | bytes 786440 | tf_op jit(solution)/shard_map/ppermute | solution.py:18
  137.7 6.7 %collective-permute-start.5 = (bf16[1024,128]{1,0:T(8,128)(2,1)S(1)}, bf16[1024,128]{1,0:T(8,128)(2,1)S(1)}, u32[]{:S(2)}, u32[]{:S(2)}) collective-permute-start(bf16[1024,128]{1,0:T(8,128)(2,1)S(1)} %fusion.52), channel_id=1, source_target_pairs={{4,0},{8,4},{12,8},{16,12},{20,16},{24,20},{28,24},{0,28},{5,1},{9... | collective-permute-start | bytes 786440 | tf_op jit(solution)/shard_map/ppermute | solution.py:19
  156.3 4.9 %copy-start.9 = (bf16[4,1,256,128]{2,3,1,0:T(8,128)(2,1)S(1)}, bf16[4,1,256,128]{2,3,1,0:T(8,128)(2,1)}, u32[]{:S(2)}) copy-start(bf16[4,1,256,128]{2,3,1,0:T(8,128)(2,1)} %copy.70) | copy-start | bytes 786436
  156.3 5.0 %copy-start.10 = (bf16[4,1,256,128]{2,3,1,0:T(8,128)(2,1)S(1)}, bf16[4,1,256,128]{2,3,1,0:T(8,128)(2,1)}, u32[]{:S(2)}) copy-start(bf16[4,1,256,128]{2,3,1,0:T(8,128)(2,1)} %copy.71) | copy-start | bytes 786436
  167.4 33.5 %copy-start = (bf16[1024,128]{1,0:T(8,128)(2,1)}, bf16[1024,128]{1,0:T(8,128)(2,1)S(1)}, u32[]{:S(2)}) copy-start(bf16[1024,128]{1,0:T(8,128)(2,1)S(1)} %fusion.48) | copy-start | bytes 786436
  167.5 8.7 %collective-permute-start.6 = (bf16[1024,128]{1,0:T(8,128)(2,1)S(1)}, bf16[1024,128]{1,0:T(8,128)(2,1)S(1)}, u32[]{:S(2)}, u32[]{:S(2)}) collective-permute-start(bf16[1024,128]{1,0:T(8,128)(2,1)S(1)} %fusion.48), channel_id=1, source_target_pairs={{0,4},{4,8},{8,12},{12,16},{16,20},{20,24},{24,28},{28,0},{1,5},{5... | collective-permute-start | bytes 786440 | tf_op jit(solution)/shard_map/ppermute | solution.py:18
  169.5 6.7 %collective-permute-start.7 = (bf16[1024,128]{1,0:T(8,128)(2,1)S(1)}, bf16[1024,128]{1,0:T(8,128)(2,1)S(1)}, u32[]{:S(2)}, u32[]{:S(2)}) collective-permute-start(bf16[1024,128]{1,0:T(8,128)(2,1)S(1)} %fusion.48), channel_id=1, source_target_pairs={{4,0},{8,4},{12,8},{16,12},{20,16},{24,20},{28,24},{0,28},{5,1},{9... | collective-permute-start | bytes 786440 | tf_op jit(solution)/shard_map/ppermute | solution.py:19
  189.9 4.9 %copy-start.11 = (bf16[4,1,256,128]{2,3,1,0:T(8,128)(2,1)S(1)}, bf16[4,1,256,128]{2,3,1,0:T(8,128)(2,1)}, u32[]{:S(2)}) copy-start(bf16[4,1,256,128]{2,3,1,0:T(8,128)(2,1)} %copy.80) | copy-start | bytes 786436
  189.9 5.0 %copy-start.12 = (bf16[4,1,256,128]{2,3,1,0:T(8,128)(2,1)S(1)}, bf16[4,1,256,128]{2,3,1,0:T(8,128)(2,1)}, u32[]{:S(2)}) copy-start(bf16[4,1,256,128]{2,3,1,0:T(8,128)(2,1)} %copy.81) | copy-start | bytes 786436
  189.9 5.0 %copy-start.6 = (bf16[4,1,256,128]{2,3,1,0:T(8,128)(2,1)S(1)}, bf16[4,1,256,128]{2,3,1,0:T(8,128)(2,1)}, u32[]{:S(2)}) copy-start(bf16[4,1,256,128]{2,3,1,0:T(8,128)(2,1)} %copy.82) | copy-start | bytes 786436
Sparse Core Ops, SparseCore 0:
  9.6 92.0 all-gather.1
where the time goes:
time: 226 us; the launch traced here: 224 us
  waiting for transfers between devices  95.2 us (42%)
  local copies, waits for them, and re-layouts  63.6 us (28%)
  matrix products  17.6 us (8%)
  between operations  14.6 us (6%)
  blocking collectives  13.9 us (6%)
  starting transfers between devices  11.7 us (5%)
  other arithmetic  7.73 us (3%)
    all_gather x1, waiting for transfers between devices, body(): full_tiles = lax.all_gather(tiles, 'probe', axis=2, tiled=True)  76.4 us
    another operation x40, local copies, waits for them, and re-layouts, body(): jnp.stack([blocks[offset:offset + row_blocks] for offset in range(offsets...  40.6 us
    unnamed x60, local copies, waits for them, and re-layouts  20 us
    dot_general x4, matrix products, body(): jnp.einsum('roij,rojp->rip', full_tiles, windows, preferred_element_type=...  17.6 us
    ppermute x4, waiting for transfers between devices, extended(): before = lax.ppermute(last, axis, up)  16.6 us
    psum x1, blocking collectives, body(): collected.append(lax.psum(local_sum, 'orb') * factor)  13.9 us
    ppermute x4, starting transfers between devices, extended(): after = lax.ppermute(initial, axis, down)  7.37 us
  transfers between devices with their start and end apart: 9, of which 6 were waited for; matrix products, arithmetic and copies ran while one was open for 5% of the time, Pallas kernels for 0%

commit v1 on v0

--- a/solution.py
+++ b/solution.py
@@ -6,6 +6,22 @@
 
 REACH = 4
 STEPS = 4
+
+
+def collect(x, axis, dim):
+    ways, here, hop = (lax.axis_size(axis), lax.axis_index(axis), x.shape[dim])
+    shape = [n * ways if d == dim else n for d, n in enumerate(x.shape)]
+    full = lax.dynamic_update_slice_in_dim(jnp.zeros(shape, x.dtype), x, here * hop, axis=dim)
+    going_up = going_down = x
+    for far in range(1, ways // 2 + 1):
+        going_up = lax.ppermute(going_up, axis, [(d, (d + 1) % ways) for d in range(ways)])
+        full = lax.dynamic_update_slice_in_dim(full, going_up, (here - far) % ways * hop, axis=dim)
+        if 2 * far < ways:
+            going_down = lax.ppermute(going_down, axis, [(d, (d - 1) % ways) for d in range(ways)])
+            full = lax.dynamic_update_slice_in_dim(
+                full, going_down, (here + far) % ways * hop, axis=dim
+            )
+    return full
 
 
 def extended(array, sides, width):
@@ -30,7 +46,7 @@
     probe_count = previous.shape[1]
     sign_f = (2 * signs - 1).astype(jnp.float32)
     factor = 1.0 / math.sqrt(lax.axis_size("orb") * row_blocks * block_rows)
-    full_tiles = lax.all_gather(tiles, "probe", axis=2, tiled=True)
+    full_tiles = collect(tiles, "probe", 2)
     mask_b = pattern.astype(jnp.bfloat16)
     older, newest = (previous, current)
     collected = []

time: 226 us -> 131 us (0.58)
  local copies, waits for them, and re-layouts: 63.6 us -> 3.78 us
  between operations: 14.6 us -> 1.12 us
  matrix products: 17.6 us -> 5.8 us
  waiting for transfers between devices: 95.2 us -> 87.7 us
  other arithmetic: 7.73 us -> 2.95 us
  starting transfers between devices: 11.7 us -> 15.8 us
    all_gather x1 -> x0, waiting for transfers between devices: 76.4 us -> none  [body(): full_tiles = lax.all_gather(tiles, 'probe', axis=2, tiled=True)]
    ppermute x0 -> x3, waiting for transfers between devices: none -> 69.3 us  [the longest x2 44.7 us: collect(): lax.ppermute(going_up, axis, [(d, (d + 1) % ways) for d in range(ways)])]
    another operation x40 -> x4, local copies, waits for them, and re-layouts: 40.6 us -> 0.15 us  [body(): jnp.stack([blocks[offset:offset + row_blocks] for offset in range(offsets...]
    unnamed x60 -> x44, local copies, waits for them, and re-layouts: 20 us -> 2.34 us
    dot_general x4, matrix products: 17.6 us -> 5.8 us  [body(): jnp.einsum('roij,rojp->rip', full_tiles, windows, preferred_element_type=...]
    ppermute x0 -> x3, starting transfers between devices: none -> 5.24 us  [the longest x2 3.08 us: collect(): lax.ppermute(going_up, axis, [(d, (d + 1) % ways) for d in range(ways)])]
    mul x4 -> x0, local copies, waits for them, and re-layouts: 2.84 us -> none  [body(): nxt = (2.0 * image - older.astype(jnp.float32)).astype(jnp.bfloat16)]
    concatenate x3, other arithmetic: 3.25 us -> 0.52 us  [extended(): array = jnp.concatenate([before, array, after], axis=dim)]
  transfers between devices with their start and end apart: 9 -> 11, of which waited for: 6 -> 8; matrix products, arithmetic and copies ran while one was open for 5% -> 2% of each run, Pallas kernels for 0% -> 0%
where the time goes in v1:
time: 131 us
  waiting for transfers between devices  87.7 us (67%)
  starting transfers between devices  15.8 us (12%)
  blocking collectives  13.5 us (10%)
  matrix products  5.8 us (4%)
  local copies, waits for them, and re-layouts  3.78 us (3%)
  other arithmetic  2.95 us (2%)
    ppermute x2, waiting for transfers between devices, collect(): lax.ppermute(going_up, axis, [(d, (d + 1) % ways) for d in range(ways)])  44.7 us
    ppermute x1, waiting for transfers between devices, collect(): lax.ppermute(going_down, axis, [(d, (d - 1) % ways) for d in range(ways)])  24.6 us
    ppermute x4, waiting for transfers between devices, extended(): before = lax.ppermute(last, axis, up)  17.2 us
    psum x1, blocking collectives, body(): collected.append(lax.psum(local_sum, 'orb') * factor)  13.5 us
    ppermute x4, starting transfers between devices, extended(): after = lax.ppermute(initial, axis, down)  6.81 us
    dot_general x4, matrix products, body(): jnp.einsum('roij,rojp->rip', full_tiles, windows, preferred_element_type=...  5.8 us
    ppermute x4, starting transfers between devices, extended(): before = lax.ppermute(last, axis, up)  3.78 us
    ppermute x2, starting transfers between devices, collect(): lax.ppermute(going_up, axis, [(d, (d + 1) % ways) for d in range(ways)])  3.08 us
  transfers between devices with their start and end apart: 11, of which 8 were waited for; matrix products, arithmetic and copies ran while one was open for 2% of the time, Pallas kernels for 0%

profile of v1, /device:TPU:0, one launch (start us, length us, event | category | flops | bytes accessed | tf_op | source)
XLA Modules:
  0.0 130.7 jit_solution(7487607436983973827)
XLA Ops:
  0.6 3.1 %collective-permute-start = (bf16[4,9,64,256]{3,2,1,0:T(8,128)(2,1)}, bf16[4,9,64,256]{3,2,1,0:T(8,128)(2,1)S(1)}, u32[]{:S(2)}, u32[]{:S(2)}) collective-permute-start(bf16[4,9,64,256]{3,2,1,0:T(8,128)(2,1)} %param.5), channel_id=1, source_target_pairs={{0,1},{1,2},{2,3},{3,0},{4,5},{5,6},{6,7},{7,4},{8,9},{9,10},{10,1... | collective-permute-start | bytes 3538952 | tf_op jit(solution)/shard_map/ppermute | solution.py:17
  3.7 0.0 collective-permute-start.3
  3.7 2.2 %collective-permute-start.1 = (bf16[4,9,64,256]{3,2,1,0:T(8,128)(2,1)}, bf16[4,9,64,256]{3,2,1,0:T(8,128)(2,1)S(1)}, u32[]{:S(2)}, u32[]{:S(2)}) collective-permute-start(bf16[4,9,64,256]{3,2,1,0:T(8,128)(2,1)} %param.5), channel_id=1, source_target_pairs={{0,3},{1,0},{2,1},{3,2},{4,7},{5,4},{6,5},{7,6},{8,11},{9,8},{10,9... | collective-permute-start | bytes 3538952 | tf_op jit(solution)/shard_map/ppermute | solution.py:20
  5.9 2.3 %collective-permute-start.4 = (bf16[1024,128]{1,0:T(8,128)(2,1)}, bf16[1024,128]{1,0:T(8,128)(2,1)S(1)}, u32[]{:S(2)}, u32[]{:S(2)}) collective-permute-start(bf16[1024,128]{1,0:T(8,128)(2,1)} %param.9), channel_id=1, source_target_pairs={{4,0},{8,4},{12,8},{16,12},{20,16},{24,20},{28,24},{0,28},{5,1},{9... | collective-permute-start | bytes 786440 | tf_op jit(solution)/shard_map/ppermute | solution.py:35
  8.2 0.7 convert_element_type.38
  8.9 0.5 broadcast_in_dim.2
  9.4 0.7 copy-done.2
  10.1 0.1 constant_dynamic-update-slice_fusion.43
  10.3 0.4 collective-permute-done.3
  10.7 0.4 copy-done.1
  11.1 0.1 constant_dynamic-update-slice_fusion.3
  11.1 1.2 collective-permute-done.4
  12.4 0.1 fusion.56
  12.6 20.2 %collective-permute-done = bf16[4,9,64,256]{3,2,1,0:T(8,128)(2,1)S(1)} collective-permute-done((bf16[4,9,64,256]{3,2,1,0:T(8,128)(2,1)}, bf16[4,9,64,256]{3,2,1,0:T(8,128)(2,1)S(1)}, u32[]{:S(2)}, u32[]{:S(2)}) %collective-permute-start) | collective-permute-done | bytes 1179680 | tf_op jit(solution)/shard_map/ppermute | solution.py:17
  32.8 0.0 collective-permute-start.2
  32.9 0.1 fusion.55
  33.2 0.1 constant_dynamic-update-slice_fusion.42
  33.3 24.6 %collective-permute-done.1 = bf16[4,9,64,256]{3,2,1,0:T(8,128)(2,1)S(1)} collective-permute-done((bf16[4,9,64,256]{3,2,1,0:T(8,128)(2,1)}, bf16[4,9,64,256]{3,2,1,0:T(8,128)(2,1)S(1)}, u32[]{:S(2)}, u32[]{:S(2)}) %collective-permute-start.1) | collective-permute-done | bytes 1179680 | tf_op jit(solution)/shard_map/ppermute | solution.py:20
  57.9 0.1 constant_dynamic-update-slice_fusion.41
  58.0 24.5 %collective-permute-done.2 = bf16[4,9,64,256]{3,2,1,0:T(8,128)(2,1)S(1)} collective-permute-done((bf16[4,9,64,256]{3,2,1,0:T(8,128)(2,1)S(1)}, bf16[4,9,64,256]{3,2,1,0:T(8,128)(2,1)S(1)}, u32[]{:S(2)}, u32[]{:S(2)}) %collective-permute-start.2) | collective-permute-done | bytes 1179680 | tf_op jit(solution)/shard_map/ppermute | solution.py:17
  82.5 0.2 constant_dynamic-update-slice_fusion.40
  82.7 0.0 copy-start.4
  82.7 1.4 %fusion.29 = f32[4,256,128]{2,1,0:T(8,128)S(1)} fusion(bf16[4,9,256,256]{3,2,1,0:T(8,128)(2,1)S(1)} %constant_dynamic-update-slice_fusion.40, bf16[4,9,256,128]{3,2,1,0:T(8,128)(2,1)S(1)} %constant_dynamic-update-slice_fusion.4, bf16[4,9]{1,0:T(4,128)(2,1)S(1)} %convert_element_type.38), kind=kOutput, calls=%fused_computation.15 | convolution fusion | flops 605290496 | bytes 7602248 | tf_op jit(solution)/shard_map/roij,rojp->rip/dot_general | solution.py:61
  84.2 0.1 fusion.41
  84.2 0.1 collective-permute-start.5
  84.3 2.6 %collective-permute-start.6 = (bf16[1024,128]{1,0:T(8,128)(2,1)S(1)}, bf16[1024,128]{1,0:T(8,128)(2,1)S(1)}, u32[]{:S(2)}, u32[]{:S(2)}) collective-permute-start(bf16[1024,128]{1,0:T(8,128)(2,1)S(1)} %fusion.41), channel_id=1, source_target_pairs={{4,0},{8,4},{12,8},{16,12},{20,16},{24,20},{28,24},{0,28},{5,1},{9... | collective-permute-start | bytes 786440 | tf_op jit(solution)/shard_map/ppermute | solution.py:35
  86.9 5.0 %collective-permute-done.5 = bf16[1024,128]{1,0:T(8,128)(2,1)S(1)} collective-permute-done((bf16[1024,128]{1,0:T(8,128)(2,1)S(1)}, bf16[1024,128]{1,0:T(8,128)(2,1)S(1)}, u32[]{:S(2)}, u32[]{:S(2)}) %collective-permute-start.5) | collective-permute-done | bytes 262176 | tf_op jit(solution)/shard_map/ppermute | solution.py:34
  91.9 0.0 collective-permute-done.6
  91.9 0.2 pad_maximum_fusion.4
  92.4 1.4 %fusion.26 = f32[4,256,128]{2,1,0:T(8,128)S(1)} fusion(bf16[4,9,256,256]{3,2,1,0:T(8,128)(2,1)S(1)} %constant_dynamic-update-slice_fusion.40, bf16[4,9,256,128]{3,2,1,0:T(8,128)(2,1)S(1)} %constant_dynamic-update-slice_fusion.13, bf16[4,9]{1,0:T(4,128)(2,1)S(1)} %convert_element_type.38), kind=kOutput, calls=%fused_computation.14 | convolution fusion | flops 605290496 | bytes 7602248 | tf_op jit(solution)/shard_map/roij,rojp->rip/dot_general | solution.py:61
  93.9 0.1 fusion.40
  94.0 1.8 %collective-permute-start.7 = (bf16[1024,128]{1,0:T(8,128)(2,1)S(1)}, bf16[1024,128]{1,0:T(8,128)(2,1)S(1)}, u32[]{:S(2)}, u32[]{:S(2)}) collective-permute-start(bf16[1024,128]{1,0:T(8,128)(2,1)S(1)} %fusion.40), channel_id=1, source_target_pairs={{0,4},{4,8},{8,12},{12,16},{16,20},{20,24},{24,28},{28,0},{1,5},{5... | collective-permute-start | bytes 786440 | tf_op jit(solution)/shard_map/ppermute | solution.py:34
  95.8 1.1 collective-permute-start.8
  96.9 5.6 %collective-permute-done.7 = bf16[1024,128]{1,0:T(8,128)(2,1)S(1)} collective-permute-done((bf16[1024,128]{1,0:T(8,128)(2,1)S(1)}, bf16[1024,128]{1,0:T(8,128)(2,1)S(1)}, u32[]{:S(2)}, u32[]{:S(2)}) %collective-permute-start.7) | collective-permute-done | bytes 262176 | tf_op jit(solution)/shard_map/ppermute | solution.py:34
  102.5 0.0 collective-permute-done.8
  102.5 0.2 pad_maximum_fusion.2
  103.0 1.4 %fusion.23 = f32[4,256,128]{2,1,0:T(8,128)S(1)} fusion(bf16[4,9,256,256]{3,2,1,0:T(8,128)(2,1)S(1)} %constant_dynamic-update-slice_fusion.40, bf16[4,9,256,128]{3,2,1,0:T(8,128)(2,1)S(1)} %constant_dynamic-update-slice_fusion.22, bf16[4,9]{1,0:T(4,128)(2,1)S(1)} %convert_element_type.38), kind=kOutput, calls=%fused_computation.13 | convolution fusion | flops 605290496 | bytes 7602248 | tf_op jit(solution)/shard_map/roij,rojp->rip/dot_general | solution.py:61
  104.5 0.1 fusion.36
  104.5 0.0 copy-start
  104.6 1.9 %collective-permute-start.9 = (bf16[1024,128]{1,0:T(8,128)(2,1)S(1)}, bf16[1024,128]{1,0:T(8,128)(2,1)S(1)}, u32[]{:S(2)}, u32[]{:S(2)}) collective-permute-start(bf16[1024,128]{1,0:T(8,128)(2,1)S(1)} %fusion.36), channel_id=1, source_target_pairs={{0,4},{4,8},{8,12},{12,16},{16,20},{20,24},{24,28},{28,0},{1,5},{5... | collective-permute-start | bytes 786440 | tf_op jit(solution)/shard_map/ppermute | solution.py:34
  106.5 0.8 collective-permute-start.10
  107.3 6.3 %collective-permute-done.9 = bf16[1024,128]{1,0:T(8,128)(2,1)S(1)} collective-permute-done((bf16[1024,128]{1,0:T(8,128)(2,1)S(1)}, bf16[1024,128]{1,0:T(8,128)(2,1)S(1)}, u32[]{:S(2)}, u32[]{:S(2)}) %collective-permute-start.9) | collective-permute-done | bytes 262176 | tf_op jit(solution)/shard_map/ppermute | solution.py:34
  113.6 0.2 pad_maximum_fusion
  114.1 0.0 copy-start.3
  114.1 1.4 %fusion.20 = f32[4,256,128]{2,1,0:T(8,128)S(1)} fusion(bf16[4,9,256,256]{3,2,1,0:T(8,128)(2,1)S(1)} %constant_dynamic-update-slice_fusion.40, bf16[4,9,256,128]{3,2,1,0:T(8,128)(2,1)S(1)} %constant_dynamic-update-slice_fusion.31, bf16[4,9]{1,0:T(4,128)(2,1)S(1)} %convert_element_type.38), kind=kOutput, calls=%fused_computation.12 | convolution fusion | flops 605290496 | bytes 7602248 | tf_op jit(solution)/shard_map/roij,rojp->rip/dot_general | solution.py:61
  115.6 1.0 fusion.37
  116.6 13.5 %all-reduce = (f32[128]{0:T(128)S(1)}, f32[128]{0:T(128)S(1)}, f32[128]{0:T(128)S(1)}, f32[128]{0:T(128)S(1)}) all-reduce(f32[128]{0:T(128)S(1)} %get-tuple-element.4, f32[128]{0:T(128)S(1)} %get-tuple-element.5, f32[128]{0:T(128)S(1)} %get-tuple-element.6, f32[128]{0:T(128)S(1)} %get-tuple-element.3), channel_id=1, replica_groups=mesh['orb'=8,'probe'=4] {'orb'}, use_global_device_ids=true, to_apply=%region_7.8 | all-reduce | flops 512 | bytes 4096 | tf_op jit(solution)/shard_map/psum | solution.py:67
  130.1 0.6 pad_maximum_fusion.6
  (47 shorter events, 1.3 us)
Async XLA Ops:
  0.6 32.2 %collective-permute-start = (bf16[4,9,64,256]{3,2,1,0:T(8,128)(2,1)}, bf16[4,9,64,256]{3,2,1,0:T(8,128)(2,1)S(1)}, u32[]{:S(2)}, u32[]{:S(2)}) collective-permute-start(bf16[4,9,64,256]{3,2,1,0:T(8,128)(2,1)} %param.5), channel_id=1, source_target_pairs={{0,1},{1,2},{2,3},{3,0},{4,5},{5,6},{6,7},{7,4},{8,9},{9,10},{10,1... | collective-permute-start | bytes 3538952 | tf_op jit(solution)/shard_map/ppermute | solution.py:17
  3.7 6.9 %collective-permute-start.3 = (bf16[1024,128]{1,0:T(8,128)(2,1)}, bf16[1024,128]{1,0:T(8,128)(2,1)S(1)}, u32[]{:S(2)}, u32[]{:S(2)}) collective-permute-start(bf16[1024,128]{1,0:T(8,128)(2,1)} %param.9), channel_id=1, source_target_pairs={{0,4},{4,8},{8,12},{12,16},{16,20},{20,24},{24,28},{28,0},{1,5},{5... | collective-permute-start | bytes 786440 | tf_op jit(solution)/shard_map/ppermute | solution.py:34
  3.7 54.1 %collective-permute-start.1 = (bf16[4,9,64,256]{3,2,1,0:T(8,128)(2,1)}, bf16[4,9,64,256]{3,2,1,0:T(8,128)(2,1)S(1)}, u32[]{:S(2)}, u32[]{:S(2)}) collective-permute-start(bf16[4,9,64,256]{3,2,1,0:T(8,128)(2,1)} %param.5), channel_id=1, source_target_pairs={{0,3},{1,0},{2,1},{3,2},{4,7},{5,4},{6,5},{7,6},{8,11},{9,8},{10,9... | collective-permute-start | bytes 3538952 | tf_op jit(solution)/shard_map/ppermute | solution.py:20
  5.9 6.5 %collective-permute-start.4 = (bf16[1024,128]{1,0:T(8,128)(2,1)}, bf16[1024,128]{1,0:T(8,128)(2,1)S(1)}, u32[]{:S(2)}, u32[]{:S(2)}) collective-permute-start(bf16[1024,128]{1,0:T(8,128)(2,1)} %param.9), channel_id=1, source_target_pairs={{4,0},{8,4},{12,8},{16,12},{20,16},{24,20},{28,24},{0,28},{5,1},{9... | collective-permute-start | bytes 786440 | tf_op jit(solution)/shard_map/ppermute | solution.py:35
  8.9 1.3 copy-start.2
  10.1 0.9 copy-start.1
  32.8 49.7 %collective-permute-start.2 = (bf16[4,9,64,256]{3,2,1,0:T(8,128)(2,1)S(1)}, bf16[4,9,64,256]{3,2,1,0:T(8,128)(2,1)S(1)}, u32[]{:S(2)}, u32[]{:S(2)}) collective-permute-start(bf16[4,9,64,256]{3,2,1,0:T(8,128)(2,1)S(1)} %collective-permute-done), channel_id=1, source_target_pairs={{0,1},{1,2},{2,3},{3,0},{4,5},{5,6},{6,7},{7,4},{8,9},{9,10},{10,1... | collective-permute-start | bytes 3538952 | tf_op jit(solution)/shard_map/ppermute | solution.py:17
  82.7 1.5 %copy-start.4 = (bf16[1024,128]{1,0:T(8,128)(2,1)S(1)}, bf16[1024,128]{1,0:T(8,128)(2,1)}, u32[]{:S(2)}) copy-start(bf16[1024,128]{1,0:T(8,128)(2,1)} %param.8) | copy-start | bytes 786436
  84.2 7.6 %collective-permute-start.5 = (bf16[1024,128]{1,0:T(8,128)(2,1)S(1)}, bf16[1024,128]{1,0:T(8,128)(2,1)S(1)}, u32[]{:S(2)}, u32[]{:S(2)}) collective-permute-start(bf16[1024,128]{1,0:T(8,128)(2,1)S(1)} %fusion.41), channel_id=1, source_target_pairs={{0,4},{4,8},{8,12},{12,16},{16,20},{20,24},{24,28},{28,0},{1,5},{5... | collective-permute-start | bytes 786440 | tf_op jit(solution)/shard_map/ppermute | solution.py:34
  84.3 7.6 %collective-permute-start.6 = (bf16[1024,128]{1,0:T(8,128)(2,1)S(1)}, bf16[1024,128]{1,0:T(8,128)(2,1)S(1)}, u32[]{:S(2)}, u32[]{:S(2)}) collective-permute-start(bf16[1024,128]{1,0:T(8,128)(2,1)S(1)} %fusion.41), channel_id=1, source_target_pairs={{4,0},{8,4},{12,8},{16,12},{20,16},{24,20},{28,24},{0,28},{5,1},{9... | collective-permute-start | bytes 786440 | tf_op jit(solution)/shard_map/ppermute | solution.py:35
  94.0 8.5 %collective-permute-start.7 = (bf16[1024,128]{1,0:T(8,128)(2,1)S(1)}, bf16[1024,128]{1,0:T(8,128)(2,1)S(1)}, u32[]{:S(2)}, u32[]{:S(2)}) collective-permute-start(bf16[1024,128]{1,0:T(8,128)(2,1)S(1)} %fusion.40), channel_id=1, source_target_pairs={{0,4},{4,8},{8,12},{12,16},{16,20},{20,24},{24,28},{28,0},{1,5},{5... | collective-permute-start | bytes 786440 | tf_op jit(solution)/shard_map/ppermute | solution.py:34
  95.8 6.7 %collective-permute-start.8 = (bf16[1024,128]{1,0:T(8,128)(2,1)S(1)}, bf16[1024,128]{1,0:T(8,128)(2,1)S(1)}, u32[]{:S(2)}, u32[]{:S(2)}) collective-permute-start(bf16[1024,128]{1,0:T(8,128)(2,1)S(1)} %fusion.40), channel_id=1, source_target_pairs={{4,0},{8,4},{12,8},{16,12},{20,16},{24,20},{28,24},{0,28},{5,1},{9... | collective-permute-start | bytes 786440 | tf_op jit(solution)/shard_map/ppermute | solution.py:35
  104.5 11.0 %copy-start = (bf16[1024,128]{1,0:T(8,128)(2,1)}, bf16[1024,128]{1,0:T(8,128)(2,1)S(1)}, u32[]{:S(2)}) copy-start(bf16[1024,128]{1,0:T(8,128)(2,1)S(1)} %fusion.36) | copy-start | bytes 786436
  104.6 9.0 %collective-permute-start.9 = (bf16[1024,128]{1,0:T(8,128)(2,1)S(1)}, bf16[1024,128]{1,0:T(8,128)(2,1)S(1)}, u32[]{:S(2)}, u32[]{:S(2)}) collective-permute-start(bf16[1024,128]{1,0:T(8,128)(2,1)S(1)} %fusion.36), channel_id=1, source_target_pairs={{0,4},{4,8},{8,12},{12,16},{16,20},{20,24},{24,28},{28,0},{1,5},{5... | collective-permute-start | bytes 786440 | tf_op jit(solution)/shard_map/ppermute | solution.py:34
  106.5 7.1 %collective-permute-start.10 = (bf16[1024,128]{1,0:T(8,128)(2,1)S(1)}, bf16[1024,128]{1,0:T(8,128)(2,1)S(1)}, u32[]{:S(2)}, u32[]{:S(2)}) collective-permute-start(bf16[1024,128]{1,0:T(8,128)(2,1)S(1)} %fusion.36), channel_id=1, source_target_pairs={{4,0},{8,4},{12,8},{16,12},{20,16},{24,20},{28,24},{0,28},{5,1},{9... | collective-permute-start | bytes 786440 | tf_op jit(solution)/shard_map/ppermute | solution.py:35
  114.1 1.5 %copy-start.3 = (s32[1024,128]{1,0:T(8,128)S(1)}, s32[1024,128]{1,0:T(8,128)}, u32[]{:S(2)}) copy-start(s32[1024,128]{1,0:T(8,128)} %param.7) | copy-start | bytes 1572868
